TPU v7x, 512 devices: a whole 4x4x16 slice. The times are simulated.
512 devices in a mesh: chain: 8 (over y, core), block: 64 (over z, x).
Axes of the slice: x: 4, y: 4, z: 16, core: 2. Of those that a mesh axis runs over, the one named last changes fastest.
Arguments:
- wave: float32 [8, 32768, 512], P('chain', 'block'), may hold values from -6 to 6
- diagonal: bfloat16 [8, 32768, 512], P('chain', 'block'), may hold values from 0.5 to 4
- left_env: bfloat16 [8, 128, 512, 512], P('chain', 'block'), may hold values from -0.125 to 0.125
- right_env: bfloat16 [8, 128, 512, 512], P('chain', 'block'), may hold values from -0.25 to 0.25
- pair_hop: int32 [128], P('block'), may hold values from 0 to 2
Outputs:
- wave_out: float32 [8, 32768, 512], P('chain', 'block')
- energies: float32 [8, 3], P('chain')
All inputs are finite; a program needn't handle non-finite values.
Results may differ from a plain program's by a relative error of at most 0.003.
Values may be sent and summed in bfloat16 or wider, within the bound.
A program may use at most 64 MiB of HBM per device.

v0:
```python
import jax
import jax.numpy as jnp
from jax import lax
from jax.sharding import PartitionSpec as P

ITERS = 3


STEP_RATE = 0.3


def from_behind(value, axis, steps):
    count = lax.axis_size(axis)
    pairs = [(source, (source + steps) % count) for source in range(count)]
    return lax.ppermute(value, axis, pairs)


def shifted(block, axis, distance):
    devices = range(lax.axis_size(axis))
    route = [(i - distance, i) for i in devices if i - distance in devices]
    return lax.ppermute(block, axis, route)


def shards(wave, diagonal, left_env, right_env, pair_hop):
    handed = from_behind(left_env, "chain", 1)
    return finish(handed, wave, diagonal, right_env, pair_hop)


def finish(handed, wave, diagonal, right_env, pair_hop):
    lefts = handed[0]
    rights = right_env[0]
    current = wave[0]
    diag_part = diagonal[0].astype(jnp.float32)
    energies = []
    for iteration in range(ITERS):
        own = current.astype(jnp.bfloat16)
        lower = shifted(own, "block", 1)
        upper = shifted(own, "block", -1)
        hops = pair_hop[:, None, None]
        inputs = jnp.where(hops == 0, lower[None], jnp.where(hops == 1, own[None], upper[None]))
        first = jnp.einsum(
            "pab,pbr->par", lefts, inputs, preferred_element_type=jnp.float32
        ).astype(jnp.bfloat16)
        terms = jnp.einsum("par,pqr->paq", first, rights, preferred_element_type=jnp.float32)
        image = jnp.sum(terms, axis=0) + diag_part * current
        product, squares = lax.psum((jnp.sum(current * image), jnp.sum(current * current)), "block")
        energy = product / squares
        current = current - STEP_RATE * (image - energy * current)
        energies.append(energy)
    return (current[None], jnp.stack(energies)[None])


def solution(mesh):
    placed = (
        P("chain", "block", None),
        P("chain", "block", None),
        P("chain", "block", None, None),
        P("chain", "block", None, None),
        P("block"),
    )
    return jax.shard_map(
        shards,
        mesh=mesh,
        in_specs=placed,
        out_specs=(P("chain", "block", None), P("chain", None)),
        check_vma=False,
    )
```

profile of v0, /device:TPU:24, one launch (start us, length us, event | category | flops | bytes accessed | tf_op | source)
XLA Modules:
  0.0 502.8 jit_solution(10339618566392483466)
XLA Ops:
  0.6 0.0 copy-start
  0.6 0.0 copy-start.1
  0.7 0.0 copy-start.9
  0.7 0.0 copy-start.4
  0.7 0.0 collective-permute-start.2
  0.7 1.8 convert_bitcast_fusion
  2.5 1.3 collective-permute-start.1
  3.8 4.6 collective-permute-start
  8.4 0.0 copy-done.9
  8.4 6.1 %collective-permute-done.1 = bf16[512,512]{1,0:T(8,128)(2,1)S(1)} collective-permute-done((bf16[512,512]{1,0:T(8,128)(2,1)S(1)}, bf16[512,512]{1,0:T(8,128)(2,1)S(1)}, u32[]{:S(2)}, u32[]{:S(2)}) %collective-permute-start.1) | collective-permute-done | bytes 524320 | tf_op jit(solution)/shard_map/ppermute | solution.py:21
  14.6 0.0 copy-start.5
  14.6 1.7 collective-permute-done
  16.3 0.0 copy-done.5
  16.3 0.0 copy-start.6
  16.3 0.0 collective-permute-done.2
  16.3 0.8 copy-done.6
  17.1 0.0 copy-done
  17.1 0.0 copy-done.1
  17.1 0.0 copy-done.4
  17.1 4.7 fusion.16
  21.8 155.1 %all-reduce.2 = (f32[]{:T(128)}, f32[]{:T(128)}) all-reduce(f32[]{:T(128)} %get-tuple-element.7, f32[]{:T(128)} %get-tuple-element.6), channel_id=1, replica_groups=mesh['chain'=8,'block'=64] {'block'}, use_global_device_ids=true, to_apply=%region_1.2 | all-reduce | flops 2 | bytes 16 | tf_op jit(solution)/shard_map/psum | solution.py:46
  178.2 1.5 fusion.62
  179.7 0.0 copy-start.3
  179.7 1.3 collective-permute-start.4
  181.0 0.0 copy-done.3
  181.0 4.6 collective-permute-start.3
  185.6 5.2 %collective-permute-done.4 = bf16[512,512]{1,0:T(8,128)(2,1)S(1)} collective-permute-done((bf16[512,512]{1,0:T(8,128)(2,1)S(1)}, bf16[512,512]{1,0:T(8,128)(2,1)S(1)}, u32[]{:S(2)}, u32[]{:S(2)}) %collective-permute-start.4) | collective-permute-done | bytes 524320 | tf_op jit(solution)/shard_map/ppermute | solution.py:21
  190.8 1.5 collective-permute-done.3
  192.3 4.7 multiply_reduce_fusion.2
  197.1 141.1 %all-reduce.1 = (f32[]{:T(128)}, f32[]{:T(128)}) all-reduce(f32[]{:T(128)} %get-tuple-element.5, f32[]{:T(128)} %get-tuple-element.4), channel_id=1, replica_groups=mesh['chain'=8,'block'=64] {'block'}, use_global_device_ids=true, to_apply=%region_5.6 | all-reduce | flops 2 | bytes 16 | tf_op jit(solution)/shard_map/psum | solution.py:46
  339.5 1.5 fusion.61
  341.0 0.0 copy-start.2
  341.0 1.3 collective-permute-start.6
  342.3 4.6 collective-permute-start.5
  346.9 5.3 %collective-permute-done.6 = bf16[512,512]{1,0:T(8,128)(2,1)S(1)} collective-permute-done((bf16[512,512]{1,0:T(8,128)(2,1)S(1)}, bf16[512,512]{1,0:T(8,128)(2,1)S(1)}, u32[]{:S(2)}, u32[]{:S(2)}) %collective-permute-start.6) | collective-permute-done | bytes 524320 | tf_op jit(solution)/shard_map/ppermute | solution.py:21
  352.1 0.0 copy-start.7
  352.1 1.5 collective-permute-done.5
  353.6 0.0 copy-done.2
  353.6 0.0 copy-done.7
  353.6 0.0 copy-start.8
  353.6 0.8 copy-done.8
  354.4 4.1 multiply_reduce_fusion
  358.5 141.1 %all-reduce = (f32[]{:T(128)}, f32[]{:T(128)}) all-reduce(f32[]{:T(128)} %get-tuple-element.3, f32[]{:T(128)} %get-tuple-element.2), channel_id=1, replica_groups=mesh['chain'=8,'block'=64] {'block'}, use_global_device_ids=true, to_apply=%region_9.10 | all-reduce | flops 2 | bytes 16 | tf_op jit(solution)/shard_map/psum | solution.py:46
  501.0 1.2 subtract_bitcast_fusion
  502.2 0.6 maximum_bitcast_fusion
  (1 shorter events, 0.0 us)
Async XLA Ops:
  0.6 16.5 %copy-start = (bf16[1,2,512,512]{3,2,1,0:T(8,128)(2,1)S(1)}, bf16[1,2,512,512]{3,2,1,0:T(8,128)(2,1)}, u32[]{:S(2)}) copy-start(bf16[1,2,512,512]{3,2,1,0:T(8,128)(2,1)} %param.8) | copy-start | bytes 3145732
  0.6 16.5 %copy-start.1 = (f32[1,512,512]{2,1,0:T(8,128)S(1)}, f32[1,512,512]{2,1,0:T(8,128)}, u32[]{:S(2)}) copy-start(f32[1,512,512]{2,1,0:T(8,128)} %param.5) | copy-start | bytes 3145732
  0.7 7.8 %copy-start.9 = (s32[2]{0:T(128)S(1)}, s32[2]{0:T(128)}, u32[]{:S(2)}) copy-start(s32[2]{0:T(128)} %param.9) | copy-start | bytes 28
  0.7 16.5 %copy-start.4 = (bf16[1,512,512]{2,1,0:T(8,128)(2,1)S(1)}, bf16[1,512,512]{2,1,0:T(8,128)(2,1)}, u32[]{:S(2)}) copy-start(bf16[1,512,512]{2,1,0:T(8,128)(2,1)} %param.6) | copy-start | bytes 1572868
  0.7 15.6 %collective-permute-start.2 = (bf16[1,2,512,512]{3,2,1,0:T(8,128)(2,1)}, bf16[1,2,512,512]{3,2,1,0:T(8,128)(2,1)}, u32[]{:S(2)}, u32[]{:S(2)}) collective-permute-start(bf16[1,2,512,512]{3,2,1,0:T(8,128)(2,1)} %param.7), channel_id=1, source_target_pairs={{0,64},{64,128},{128,192},{192,256},{256,320},{320,384},{384,448},... | collective-permute-start | bytes 3145736 | tf_op jit(solution)/shard_map/ppermute | solution.py:15
  2.5 12.0 %collective-permute-start.1 = (bf16[512,512]{1,0:T(8,128)(2,1)S(1)}, bf16[512,512]{1,0:T(8,128)(2,1)S(1)}, u32[]{:S(2)}, u32[]{:S(2)}) collective-permute-start(bf16[512,512]{1,0:T(8,128)(2,1)S(1)} %get-tuple-element.19), channel_id=1, source_target_pairs={{1,0},{2,1},{3,2},{4,3},{5,4},{6,5},{7,6},{8,7},{9,8},{10,9},{11,1... | collective-permute-start | bytes 1572872 | tf_op jit(solution)/shard_map/ppermute | solution.py:21
  3.8 12.5 %collective-permute-start = (bf16[512,512]{1,0:T(8,128)(2,1)S(1)}, bf16[512,512]{1,0:T(8,128)(2,1)S(1)}, u32[]{:S(2)}, u32[]{:S(2)}) collective-permute-start(bf16[512,512]{1,0:T(8,128)(2,1)S(1)} %get-tuple-element.19), channel_id=1, source_target_pairs={{0,1},{1,2},{2,3},{3,4},{4,5},{5,6},{6,7},{7,8},{8,9},{9,10},{10,1... | collective-permute-start | bytes 1572872 | tf_op jit(solution)/shard_map/ppermute | solution.py:21
  14.6 1.7 copy-start.5
  16.3 0.8 copy-start.6
  179.7 1.3 copy-start.3
  179.7 11.1 %collective-permute-start.4 = (bf16[512,512]{1,0:T(8,128)(2,1)S(1)}, bf16[512,512]{1,0:T(8,128)(2,1)S(1)}, u32[]{:S(2)}, u32[]{:S(2)}) collective-permute-start(bf16[512,512]{1,0:T(8,128)(2,1)S(1)} %get-tuple-element.16), channel_id=1, source_target_pairs={{1,0},{2,1},{3,2},{4,3},{5,4},{6,5},{7,6},{8,7},{9,8},{10,9},{11,1... | collective-permute-start | bytes 1572872 | tf_op jit(solution)/shard_map/ppermute | solution.py:21
  181.0 11.3 %collective-permute-start.3 = (bf16[512,512]{1,0:T(8,128)(2,1)S(1)}, bf16[512,512]{1,0:T(8,128)(2,1)S(1)}, u32[]{:S(2)}, u32[]{:S(2)}) collective-permute-start(bf16[512,512]{1,0:T(8,128)(2,1)S(1)} %get-tuple-element.16), channel_id=1, source_target_pairs={{0,1},{1,2},{2,3},{3,4},{4,5},{5,6},{6,7},{7,8},{8,9},{9,10},{10,1... | collective-permute-start | bytes 1572872 | tf_op jit(solution)/shard_map/ppermute | solution.py:21
  341.0 12.6 %copy-start.2 = (bf16[512,512]{1,0:T(8,128)(2,1)}, bf16[512,512]{1,0:T(8,128)(2,1)S(1)}, u32[]{:S(2)}) copy-start(bf16[512,512]{1,0:T(8,128)(2,1)S(1)} %get-tuple-element.14) | copy-start | bytes 1572868
  341.0 11.2 %collective-permute-start.6 = (bf16[512,512]{1,0:T(8,128)(2,1)S(1)}, bf16[512,512]{1,0:T(8,128)(2,1)S(1)}, u32[]{:S(2)}, u32[]{:S(2)}) collective-permute-start(bf16[512,512]{1,0:T(8,128)(2,1)S(1)} %get-tuple-element.14), channel_id=1, source_target_pairs={{1,0},{2,1},{3,2},{4,3},{5,4},{6,5},{7,6},{8,7},{9,8},{10,9},{11,1... | collective-permute-start | bytes 1572872 | tf_op jit(solution)/shard_map/ppermute | solution.py:21
  342.3 11.3 %collective-permute-start.5 = (bf16[512,512]{1,0:T(8,128)(2,1)S(1)}, bf16[512,512]{1,0:T(8,128)(2,1)S(1)}, u32[]{:S(2)}, u32[]{:S(2)}) collective-permute-start(bf16[512,512]{1,0:T(8,128)(2,1)S(1)} %get-tuple-element.14), channel_id=1, source_target_pairs={{0,1},{1,2},{2,3},{3,4},{4,5},{5,6},{6,7},{7,8},{8,9},{9,10},{10,1... | collective-permute-start | bytes 1572872 | tf_op jit(solution)/shard_map/ppermute | solution.py:21
  352.1 1.5 copy-start.7
  353.6 0.8 copy-start.8
where the time goes:
time: 507 us; the launch traced here: 503 us
  blocking collectives  437 us (86%)
  waiting for transfers between devices  21.3 us (4%)
  starting transfers between devices  17.6 us (3%)
  matrix products  13.5 us (3%)
  other arithmetic  6.61 us (1%)
    psum x3, blocking collectives, finish(): lax.psum((jnp.sum(current * image), jnp.sum(current * current)), 'block')  437 us
    ppermute x6, waiting for transfers between devices, shifted(): return lax.ppermute(block, axis, route)  21.3 us
    ppermute x6, starting transfers between devices, shifted(): return lax.ppermute(block, axis, route)  17.6 us
    dot_general x3, matrix products, finish(): jnp.einsum('par,pqr->paq', first, rights, preferred_element_type=jnp.floa...  13.5 us
  transfers between devices with their start and end apart: 7, of which 6 were waited for; matrix products, arithmetic and copies ran while one was open for 0% of the time, Pallas kernels for 0%

commit v1 on v0

v1 whole, which is shorter than its diff:
```python
import functools

import jax
import jax.numpy as jnp
from jax import lax
from jax.experimental import pallas as pl
from jax.experimental.pallas import tpu as pltpu
from jax.sharding import PartitionSpec as P

MESH = pl.DeviceIdType.MESH
BS = 512
ITERS = 3
RATE = 0.3
FIRST_SHIFT = 2.0
NCH = 4
CW = BS // NCH
XG = 4
F32 = jnp.float32
BF16 = jnp.bfloat16


def dot(a, b):
    return jnp.dot(a, b, preferred_element_type=F32)


def fold(values):
    return jnp.sum(values.reshape(BS // 8, 8, CW), axis=0)


def kernel(segs, nblk, *refs):
    (hop_hbm, wave_hbm, diag_hbm, left_hbm, right_hbm, out_hbm, en_ref) = refs[:7]
    refs = refs[7:]
    bufs = refs[: ITERS * NCH]
    refs = refs[ITERS * NCH:]
    (hop_s, x_v, diag_v, right_v, left_v, rt_v, d_v, dprev_v, c_v, b_v, im_v, out_v,
     xpart, zpart, in_sem, out_sem, l_send, l_recv, x_send, x_recv, s1_send, s1_recv, s2_send, s2_recv) = refs

    zg = nblk // XG
    c = lax.axis_index("chain")
    j = lax.axis_index("block")
    zi, xi = j // XG, j % XG
    up, down = (j + 1) % nblk, (j + nblk - 1) % nblk
    after, before = (c + 1) % segs, (c + segs - 1) % segs
    x_others = [zi * XG + (xi + d) % XG for d in range(1, XG)]
    x_slots = [(xi + d) % XG for d in range(1, XG)]
    z_others = [((zi + d) % zg) * XG + xi for d in range(1, zg)]
    z_slots = [(zi + d) % zg for d in range(1, zg)]

    barrier = pltpu.get_barrier_semaphore()
    partners = [{"block": t} for t in [up, down] + x_others + z_others] + [{"chain": t} for t in (after, before)]
    for device in partners:
        pl.semaphore_signal(barrier, inc=1, device_id=device, device_id_type=MESH)

    def load(source, target, index):
        copy = pltpu.make_async_copy(source, target, in_sem.at[index])
        copy.start()
        return copy

    wave_in = load(wave_hbm.at[0], x_v, 0)
    right_in = load(right_hbm.at[0], right_v, 1)
    diag_in = load(diag_hbm.at[0], diag_v, 2)
    hop_in = load(hop_hbm, hop_s, 3)

    def piece(s):
        return s // 2, pl.ds((s % 2) * (BS // 2), BS // 2)

    l_copies = []
    for s in range(4):
        p, rows = piece(s)
        l_copies.append(pltpu.make_async_remote_copy(
            src_ref=left_hbm.at[0, p, rows], dst_ref=left_v.at[p, rows],
            send_sem=l_send.at[s], recv_sem=l_recv.at[s], device_id={"chain": after}, device_id_type=MESH))

    def exchange(k, q):
        buf = bufs[k * NCH + q]
        copies = []
        for way, (slot, target) in enumerate(((0, up), (2, down))):
            copies.append(pltpu.make_async_remote_copy(
                src_ref=buf.at[1], dst_ref=buf.at[slot], send_sem=x_send.at[k, q, way], recv_sem=x_recv.at[k, q, way],
                device_id={"block": target}, device_id_type=MESH))
        return copies

    moves = [[exchange(k, q) for q in range(NCH)] for k in range(ITERS)]

    def columns(q):
        return pl.ds(q * CW, CW)

    wave_in.wait()
    for q in range(NCH):
        bufs[q][1] = x_v[:, columns(q)].astype(BF16)
    pl.semaphore_wait(barrier, len(partners))
    for copy in l_copies:
        copy.start()
    for q in range(NCH):
        for copy in moves[0][q]:
            copy.start()

    hop_in.wait()
    hops = [hop_s[p] for p in range(2)]
    right_in.wait()
    for p in range(2):
        source = j + hops[p] - 1
        inside = jnp.logical_and(source >= 0, source < nblk)
        rights = right_v[p].astype(F32) * jnp.where(inside, 1.0, 0.0).astype(F32)
        rt_v[p] = rights.T.astype(BF16)
    diag_in.wait()

    def prepare(shift):
        squares = jnp.zeros((8, CW), F32)
        for q in range(NCH):
            x = x_v[:, columns(q)]
            known = diag_v[:, columns(q)].astype(F32) * x
            c_v[:, columns(q)] = known
            b_v[:, columns(q)] = (1.0 + RATE * shift) * x - RATE * known
            squares += fold(x * x)
        return squares

    def update(energy, shift):
        squares = jnp.zeros((8, CW), F32)
        gap = RATE * (energy - shift)
        for q in range(NCH):
            x = x_v[:, columns(q)]
            x = x - RATE * (im_v[:, columns(q)] - energy * x)
            known = diag_v[:, columns(q)].astype(F32) * x + gap * dprev_v[:, columns(q)]
            x_v[:, columns(q)] = x
            c_v[:, columns(q)] = known
            b_v[:, columns(q)] = (1.0 + RATE * energy) * x - RATE * known
            squares += fold(x * x)
        return squares, gap

    def sums_start(k, product, squares):
        xpart[k, xi, 0:1] = jnp.sum(product, axis=0, keepdims=True)
        xpart[k, xi, 1:2] = jnp.sum(squares, axis=0, keepdims=True)
        copies = []
        for d, target in enumerate(x_others):
            copies.append(pltpu.make_async_remote_copy(
                src_ref=xpart.at[k, xi], dst_ref=xpart.at[k, xi], send_sem=s1_send.at[k, d], recv_sem=s1_recv.at[k, xi],
                device_id={"block": target}, device_id_type=MESH))
        for copy in copies:
            copy.start()
        return copies

    def sums_middle(k):
        for slot in x_slots:
            pltpu.make_async_copy(xpart.at[k, slot], xpart.at[k, slot], s1_recv.at[k, slot]).wait()
        total = xpart[k, 0]
        for slot in range(1, XG):
            total += xpart[k, slot]
        zpart[k, zi] = total
        copies = []
        for d, target in enumerate(z_others):
            copies.append(pltpu.make_async_remote_copy(
                src_ref=zpart.at[k, zi], dst_ref=zpart.at[k, zi], send_sem=s2_send.at[k, d], recv_sem=s2_recv.at[k, zi],
                device_id={"block": target}, device_id_type=MESH))
        for copy in copies:
            copy.start()
        return copies

    def sums_end(k):
        for slot in z_slots:
            pltpu.make_async_copy(zpart.at[k, slot], zpart.at[k, slot], s2_recv.at[k, slot]).wait()
        total = zpart[k, 0]
        for slot in range(1, zg):
            total += zpart[k, slot]
        total = jnp.sum(total, axis=1, keepdims=True)
        energy = total[0:1] / total[1:2]
        en_ref[0:1, k:k + 1] = energy
        return energy

    def arrived(k, q):
        for copy in moves[k][q]:
            copy.wait_recv()

    pending = []
    shift = FIRST_SHIFT
    gap = None
    squares = prepare(shift)
    for k in range(ITERS):
        last = None
        if k == 0:
            for s in range(NCH):
                arrived(0, s)
                l_copies[s].wait_recv()
                for t in range(s + 1):
                    p, rows = piece(t)
                    firsts = range(s + 1) if t == s else [s]
                    first = [dot(left_v[p, rows], bufs[q][hops[p]]).astype(BF16) for q in firsts]
                    first = jnp.concatenate(first, axis=1)
                    depth = pl.ds(firsts[0] * CW, len(firsts) * CW)
                    more = dot(first, rt_v[p, depth])
                    if s == 0:
                        d_v[rows] = more
                    elif t == s and s == 1:
                        d_v[rows] = more
                    else:
                        d_v[rows] = d_v[rows] + more
        else:
            for q in range(NCH):
                arrived(k, q)
                first = [dot(left_v[p], bufs[k * NCH + q][hops[p]]).astype(BF16) for p in range(2)]
                first = jnp.concatenate(first, axis=1)
                if q == NCH - 1:
                    last = first
                    break
                more = dot(first, jnp.concatenate([rt_v[p, columns(q)] for p in range(2)], axis=0))
                d_v[...] = more if q == 0 else d_v[...] + more
                if q == 0:
                    pending += sums_middle(k - 1)
                if q == 1:
                    energy = sums_end(k - 1)
                    squares, gap = update(energy, shift)
                    shift = energy
        for half in range(2):
            wide = pl.ds(half * 2 * CW, 2 * CW)
            if last is not None:
                rights = jnp.concatenate([rt_v[p, columns(NCH - 1), wide] for p in range(2)], axis=0)
                d_v[:, wide] = d_v[:, wide] + dot(last, rights)
            if k < ITERS - 1:
                for q in (2 * half, 2 * half + 1):
                    y = b_v[:, columns(q)] - RATE * d_v[:, columns(q)]
                    bufs[(k + 1) * NCH + q][1] = y.astype(BF16)
                    for copy in moves[k + 1][q]:
                        copy.start()
        product = jnp.zeros((8, CW), F32)
        for q in range(NCH):
            d = d_v[:, columns(q)]
            image = d + c_v[:, columns(q)]
            im_v[:, columns(q)] = image
            product += fold(x_v[:, columns(q)] * image)
        pending += sums_start(k, product, squares)
        if k < ITERS - 1:
            for q in range(NCH):
                d = d_v[:, columns(q)]
                dprev_v[:, columns(q)] = d if gap is None else d + gap * dprev_v[:, columns(q)]

    pending += sums_middle(ITERS - 1)
    energy = sums_end(ITERS - 1)
    outs = []
    for q in range(NCH):
        x = x_v[:, columns(q)]
        out_v[:, columns(q)] = x - RATE * (im_v[:, columns(q)] - energy * x)
    out = pltpu.make_async_copy(out_v, out_hbm.at[0], out_sem)
    out.start()
    for copy in pending + l_copies + [m for step in moves for pair in step for m in pair]:
        copy.wait_send()
    out.wait()


def shards(wave, diagonal, left_env, right_env, pair_hop, segs, nblk):
    zg = nblk // XG
    dma = pltpu.SemaphoreType.DMA
    square = pltpu.VMEM((BS, BS), F32)
    anywhere = pl.BlockSpec(memory_space=pl.ANY)
    return pl.pallas_call(
        functools.partial(kernel, segs, nblk),
        out_shape=(
            jax.ShapeDtypeStruct((1, BS, BS), F32),
            jax.ShapeDtypeStruct((1, ITERS), F32),
        ),
        in_specs=[anywhere] * 5,
        out_specs=(anywhere, pl.BlockSpec(memory_space=pltpu.VMEM)),
        scratch_shapes=[pltpu.VMEM((3, BS, CW), BF16)] * (ITERS * NCH) + [
            pltpu.SMEM((2,), jnp.int32),
            square,
            pltpu.VMEM((BS, BS), BF16),
            pltpu.VMEM((2, BS, BS), BF16),
            pltpu.VMEM((2, BS, BS), BF16),
            pltpu.VMEM((2, BS, BS), BF16),
            square, square, square, square, square, square,
            pltpu.VMEM((ITERS, XG, 2, 128), F32),
            pltpu.VMEM((ITERS, zg, 2, 128), F32),
            dma((4,)),
            dma(()),
            dma((4,)),
            dma((4,)),
            dma((ITERS, NCH, 2)),
            dma((ITERS, NCH, 2)),
            dma((ITERS, XG - 1)),
            dma((ITERS, XG)),
            dma((ITERS, max(zg - 1, 1))),
            dma((ITERS, zg)),
        ],
        compiler_params=pltpu.CompilerParams(
            collective_id=0, has_side_effects=True, vmem_limit_bytes=48 * 2 ** 20),
        cost_estimate=pl.CostEstimate(flops=ITERS * 8 * BS ** 3, bytes_accessed=9 * 2 ** 19, transcendentals=0),
    )(pair_hop, wave, diagonal, left_env, right_env)


def solution(mesh):
    placed = (
        P("chain", "block", None),
        P("chain", "block", None),
        P("chain", "block", None, None),
        P("chain", "block", None, None),
        P("block"),
    )
    return jax.shard_map(
        functools.partial(shards, segs=mesh.shape["chain"], nblk=mesh.shape["block"]),
        mesh=mesh,
        in_specs=placed,
        out_specs=(P("chain", "block", None), P("chain", None)),
        check_vma=False,
    )
```

time: 507 us -> 92.7 us (0.18)
  blocking collectives: 437 us -> 0 us
  Pallas kernels: 0 us -> 84.9 us
  waiting for transfers between devices: 21.3 us -> 0 us
  starting transfers between devices: 17.6 us -> 0 us
  matrix products: 13.5 us -> 0 us
  other arithmetic: 6.61 us -> 0 us
  local copies, waits for them, and re-layouts: 1.65 us -> 6.84 us
    psum x3 -> x0, blocking collectives: 437 us -> none  [finish(): lax.psum((jnp.sum(current * image), jnp.sum(current * current)), 'block')]
    pallas_call x0 -> x1, Pallas kernels: none -> 84.9 us  [shards(): pl.pallas_call(functools.partial(kernel, segs, nblk), out_shape=(jax.Shap...]
    ppermute x7 -> x0, waiting for transfers between devices: 21.3 us -> none  [the longest x6 21.3 us: shifted(): return lax.ppermute(block, axis, route)]
    ppermute x7 -> x0, starting transfers between devices: 17.6 us -> none  [the longest x6 17.6 us: shifted(): return lax.ppermute(block, axis, route)]
    dot_general x3 -> x0, matrix products: 13.5 us -> none  [finish(): jnp.einsum('par,pqr->paq', first, rights, preferred_element_type=jnp.floa...]
    unnamed x20 -> x12, local copies, waits for them, and re-layouts: 1.65 us -> 6.84 us
  transfers between devices with their start and end apart: 7 -> 0, of which waited for: 6 -> 0; matrix products, arithmetic and copies ran while one was open for 0% -> 0% of each run, Pallas kernels for 0% -> 0%
where the time goes in v1:
time: 92.7 us; the launch traced here: 92.4 us
  Pallas kernels  84.9 us (92%)
  local copies, waits for them, and re-layouts  6.84 us (7%)
    pallas_call x1, Pallas kernels, shards(): pl.pallas_call(functools.partial(kernel, segs, nblk), out_shape=(jax.Shap...  84.9 us
    unnamed x12, local copies, waits for them, and re-layouts  6.84 us

profile of v1, /device:TPU:24, one launch (start us, length us, event | category | flops | bytes accessed | tf_op | source)
XLA Modules:
  0.0 92.4 jit_solution(5753495511323332405)
XLA Ops:
  0.6 0.0 copy-start
  0.6 1.2 %copy-done = f32[1,512,512]{2,1,0:T(8,128)S(1)} copy-done((f32[1,512,512]{2,1,0:T(8,128)S(1)}, f32[1,512,512]{2,1,0:T(8,128)}, u32[]{:S(2)}) %copy-start) | copy-done | bytes 1048600
  1.9 0.0 copy-start.1
  1.9 1.2 %copy-done.1 = bf16[1,2,512,512]{3,2,1,0:T(8,128)(2,1)S(1)} copy-done((bf16[1,2,512,512]{3,2,1,0:T(8,128)(2,1)S(1)}, bf16[1,2,512,512]{3,2,1,0:T(8,128)(2,1)}, u32[]{:S(2)}) %copy-start.1) | copy-done | bytes 1048600
  3.1 0.0 copy-start.2
  3.1 1.2 %copy-done.2 = bf16[1,2,512,512]{3,2,1,0:T(8,128)(2,1)S(1)} copy-done((bf16[1,2,512,512]{3,2,1,0:T(8,128)(2,1)S(1)}, bf16[1,2,512,512]{3,2,1,0:T(8,128)(2,1)}, u32[]{:S(2)}) %copy-start.2) | copy-done | bytes 1048600
  4.3 0.0 copy-start.3
  4.3 1.0 %copy-done.3 = bf16[1,512,512]{2,1,0:T(8,128)(2,1)S(1)} copy-done((bf16[1,512,512]{2,1,0:T(8,128)(2,1)S(1)}, bf16[1,512,512]{2,1,0:T(8,128)(2,1)}, u32[]{:S(2)}) %copy-start.3) | copy-done | bytes 524312
  5.3 0.0 copy-start.4
  5.4 0.7 copy-done.4
  6.0 84.9 %shard_map.68 = (f32[1,512,512]{2,1,0:T(8,128)S(1)}, f32[1,3]{1,0:T(1,128)S(1)}) custom-call(s32[2]{0:T(128)S(1)} %copy-done.4, f32[1,512,512]{2,1,0:T(8,128)S(1)} %copy-done, bf16[1,512,512]{2,1,0:T(8,128)(2,1)S(1)} %copy-done.3, bf16[1,2,512,512]{3,2,1,0:T(8,128)(2,1)S(1)} %copy-done.1, bf16[1,2,512,512]{3,2,1,0:T(8,128)(2,1)S(1)} %copy-done.2), custom_call_target="tpu_custom_call" | custom-call | flops 3221225472 | bytes 4718592 | tf_op jit(solution)/shard_map/pallas_call | solution.py:254
  90.9 1.0 %copy.9 = f32[1,512,512]{2,1,0:T(8,128)} copy(f32[1,512,512]{2,1,0:T(8,128)S(1)} %get-tuple-element.4) | data formatting | bytes 2097152
  91.9 0.5 copy.10
Async XLA Ops:
  0.6 1.2 %copy-start = (f32[1,512,512]{2,1,0:T(8,128)S(1)}, f32[1,512,512]{2,1,0:T(8,128)}, u32[]{:S(2)}) copy-start(f32[1,512,512]{2,1,0:T(8,128)} %refs_1_.1) | copy-start | bytes 3145732
  1.9 1.2 %copy-start.1 = (bf16[1,2,512,512]{3,2,1,0:T(8,128)(2,1)S(1)}, bf16[1,2,512,512]{3,2,1,0:T(8,128)(2,1)}, u32[]{:S(2)}) copy-start(bf16[1,2,512,512]{3,2,1,0:T(8,128)(2,1)} %refs_3_.1) | copy-start | bytes 3145732
  3.1 1.2 %copy-start.2 = (bf16[1,2,512,512]{3,2,1,0:T(8,128)(2,1)S(1)}, bf16[1,2,512,512]{3,2,1,0:T(8,128)(2,1)}, u32[]{:S(2)}) copy-start(bf16[1,2,512,512]{3,2,1,0:T(8,128)(2,1)} %refs_4_.1) | copy-start | bytes 3145732
  4.3 1.0 %copy-start.3 = (bf16[1,512,512]{2,1,0:T(8,128)(2,1)S(1)}, bf16[1,512,512]{2,1,0:T(8,128)(2,1)}, u32[]{:S(2)}) copy-start(bf16[1,512,512]{2,1,0:T(8,128)(2,1)} %refs_2_.1) | copy-start | bytes 1572868
  5.3 0.7 copy-start.4

commit v2 on v1

v2 whole, which is shorter than its diff:
```python
import functools

import jax
import jax.numpy as jnp
from jax import lax
from jax.experimental import pallas as pl
from jax.experimental.pallas import tpu as pltpu
from jax.sharding import PartitionSpec as P

MESH = pl.DeviceIdType.MESH
BS = 512
ITERS = 3
RATE = 0.3
SHIFT = 1.5
PAIRS = ((0, 0), (0, 1), (1, 1), (0, 2), (1, 2), (2, 2), (0, 3), (1, 3), (2, 3))
NCH = 4
CW = BS // NCH
XG = 4
F32 = jnp.float32
BF16 = jnp.bfloat16


def dot(a, b):
    return jnp.dot(a, b, preferred_element_type=F32)


def fold(values):
    return jnp.sum(values.reshape(BS // 8, 8, CW), axis=0)


def kernel(segs, nblk, *refs):
    (hop_hbm, wave_hbm, diag_hbm, left_hbm, right_hbm, out_ref, en_ref) = refs[:7]
    ys = refs[7:11]
    refs = refs[11:]
    bufs = refs[: ITERS * NCH]
    refs = refs[ITERS * NCH:]
    (hop_s, diag_v, right_v, left_v, rt_v, d_v, m_v,
     parts, in_sem, l_send, l_recv, x_send, x_recv, sum_sems, near_sem) = refs

    zg = nblk // XG
    c = lax.axis_index("chain")
    j = lax.axis_index("block")
    zi, xi = j // XG, j % XG
    up, down = (j + 1) % nblk, (j + nblk - 1) % nblk
    after, before = (c + 1) % segs, (c + segs - 1) % segs
    even = c % 2 == 0

    def block_at(dz, dx):
        return {"block": (zi + dz) % zg * XG + (xi + dx) % XG}

    def far(offset):
        dz, dx = offset
        return min(dz, zg - dz) + min(dx, XG - dx)

    others = [(dz, dx) for dz in range(zg) for dx in range(XG) if (dz, dx) != (0, 0)]
    others = sorted(others, key=far, reverse=True)

    barrier = pltpu.get_barrier_semaphore()
    partners = [{"block": up}, {"block": down}] + [block_at(0, dx) for dx in range(1, XG)]
    partners += [block_at(1, 0), block_at(zg - 1, 0), {"chain": after}, {"chain": before}]
    for device in partners:
        pl.semaphore_signal(barrier, inc=1, device_id=device, device_id_type=MESH)

    reaches = [1 << r for r in range(zg.bit_length() - 1)]

    def near_start(r):
        for dz in {reaches[r], zg - reaches[r]}:
            pl.semaphore_signal(near_sem.at[r], inc=1, device_id=block_at(dz, 0), device_id_type=MESH)

    def near_next(r):
        if r < len(reaches):
            pl.semaphore_wait(near_sem.at[r], len({reaches[r], zg - reaches[r]}))
        if r + 1 < len(reaches):
            near_start(r + 1)

    def load(source, target, index):
        copy = pltpu.make_async_copy(source, target, in_sem.at[index])
        copy.start()
        return copy

    def columns(q):
        return pl.ds(q * CW, CW)

    wave_in = [load(wave_hbm.at[0, :, columns(q)], ys[0].at[:, columns(q)], q) for q in range(NCH)]
    right_in = load(right_hbm.at[0], right_v, NCH)
    diag_in = load(diag_hbm.at[0], diag_v, NCH + 1)
    hop_in = load(hop_hbm, hop_s, NCH + 2)

    def piece(s):
        return s // 2, pl.ds((s % 2) * (BS // 2), BS // 2)

    l_copies = []
    for s in range(4):
        p, rows = piece(s)
        l_copies.append(pltpu.make_async_remote_copy(
            src_ref=left_hbm.at[0, p, rows], dst_ref=left_v.at[p, rows],
            send_sem=l_send.at[s], recv_sem=l_recv.at[s], device_id={"chain": after}, device_id_type=MESH))

    def exchange(k, q):
        buf = bufs[k * NCH + q]
        copies = []
        for way, (slot, target) in enumerate(((0, up), (2, down))):
            copies.append(pltpu.make_async_remote_copy(
                src_ref=buf.at[1], dst_ref=buf.at[slot], send_sem=x_send.at[k, q, way], recv_sem=x_recv.at[k, q, way],
                device_id={"block": target}, device_id_type=MESH))
        return copies

    moves = [[exchange(k, q) for q in range(NCH)] for k in range(ITERS)]

    pl.semaphore_wait(barrier, len(partners))
    for copy in l_copies:
        copy.start()
    for q in range(NCH):
        wave_in[q].wait()
        bufs[q][1] = ys[0][:, columns(q)].astype(BF16)
        for copy in moves[0][q]:
            copy.start()
    near_start(0)

    hop_in.wait()
    hops = [hop_s[p] for p in range(2)]
    right_in.wait()
    for p in range(2):
        source = j + hops[p] - 1
        inside = jnp.logical_and(source >= 0, source < nblk)
        rights = right_v[p].astype(F32) * jnp.where(inside, 1.0, 0.0).astype(F32)
        rt_v[p] = rights.T.astype(BF16)
    diag_in.wait()

    for q in range(NCH):
        m_v[:, columns(q)] = (1.0 + RATE * SHIFT) - RATE * diag_v[:, columns(q)].astype(F32)

    lane = lax.broadcasted_iota(jnp.int32, (1, CW), 1)

    def inner(a, b):
        total = jnp.zeros((8, CW), F32)
        for q in range(NCH):
            total += fold(ys[a][:, columns(q)] * ys[b][:, columns(q)])
        return total

    def placed(pair, total):
        total = jnp.sum(jnp.sum(total, axis=0, keepdims=True), axis=1, keepdims=True)
        return jnp.where(lane == PAIRS.index(pair), total, 0.0)

    every = parts.at[pl.ds(0, nblk - 1)]

    def sums_start(row):
        parts[j] = row
        for dz, dx in others:
            pltpu.make_async_remote_copy(
                src_ref=parts.at[j], dst_ref=parts.at[j], send_sem=sum_sems.at[0], recv_sem=sum_sems.at[1],
                device_id=block_at(dz, dx), device_id_type=MESH).start()

    def arrived(k, q):
        for copy in moves[k][q]:
            copy.wait_recv()

    def first_terms(t, chunks, begin=False):
        p, rows = piece(t)
        first = [dot(left_v[p, rows], bufs[q][hops[p]]).astype(BF16) for q in chunks]
        first = jnp.concatenate(first, axis=1)
        more = dot(first, rt_v[p, pl.ds(chunks[0] * CW, len(chunks) * CW)])
        d_v[rows] = more if begin else d_v[rows] + more

    row = jnp.zeros((1, CW), F32)
    last_sums = [jnp.zeros((8, CW), F32)] * ITERS
    for k in range(ITERS):
        last = None
        if k == 0:
            for s in range(NCH - 1):
                arrived(0, s)
                l_copies[s].wait_recv()
                near_next(s)
                for t in range(s + 1):
                    first_terms(t, range(s + 1) if t == s else [s], t == s and s < 2)

            @pl.when(even)
            def _():
                arrived(0, NCH - 1)
                for t in range(NCH - 1):
                    first_terms(t, [NCH - 1])
                l_copies[NCH - 1].wait_recv()
                first_terms(NCH - 1, range(NCH))

            @pl.when(jnp.logical_not(even))
            def _():
                l_copies[NCH - 1].wait_recv()
                first_terms(NCH - 1, range(NCH - 1))
                arrived(0, NCH - 1)
                for t in range(NCH):
                    first_terms(t, [NCH - 1])

        else:
            for q in range(NCH):
                arrived(k, q)
                first = [dot(left_v[p], bufs[k * NCH + q][hops[p]]).astype(BF16) for p in range(2)]
                first = jnp.concatenate(first, axis=1)
                if q == NCH - 1:
                    last = first
                    break
                more = dot(first, jnp.concatenate([rt_v[p, columns(q)] for p in range(2)], axis=0))
                d_v[...] = more if q == 0 else d_v[...] + more
        for half in range(2):
            wide = pl.ds(half * 2 * CW, 2 * CW)
            if last is not None:
                rights = jnp.concatenate([rt_v[p, columns(NCH - 1), wide] for p in range(2)], axis=0)
                d_v[:, wide] = d_v[:, wide] + dot(last, rights)
            for q in (2 * half, 2 * half + 1):
                y = m_v[:, columns(q)] * ys[k][:, columns(q)] - RATE * d_v[:, columns(q)]
                ys[k + 1][:, columns(q)] = y
                if k < ITERS - 1:
                    bufs[(k + 1) * NCH + q][1] = y.astype(BF16)
                    for copy in moves[k + 1][q]:
                        copy.start()
                else:
                    for a in range(ITERS):
                        last_sums[a] += fold(ys[a][:, columns(q)] * y)
        if k < ITERS - 1:
            for pair in PAIRS:
                if pair[1] == k + 1 or (k == 0 and pair == (0, 0)):
                    row = row + placed(pair, inner(*pair))
    for r in range(NCH - 1, len(reaches)):
        near_next(r)
    for a in range(ITERS):
        row = row + placed((a, ITERS), last_sums[a])
    sums_start(row)
    for copy in l_copies + [m for step in moves for pair in step for m in pair]:
        copy.wait_send()
    pltpu.make_async_copy(every, every, sum_sems.at[1]).wait()
    total = jnp.sum(parts[...], axis=0)
    g = {}
    for i, (a, b) in enumerate(PAIRS):
        g[a, b] = total[0:1, i:i + 1]
    b0 = 1.0 - g[0, 1] / g[0, 0]
    squares = g[1, 1] + b0 * (2.0 * g[0, 1] + b0 * g[0, 0])
    b1 = 1.0 - (g[1, 2] + b0 * (g[1, 1] + g[0, 2] + b0 * g[0, 1])) / squares
    s, t = b0 + b1, b0 * b1
    squares = g[2, 2] + s * (2.0 * g[1, 2] + s * g[1, 1] + 2.0 * t * g[0, 1]) + t * (2.0 * g[0, 2] + t * g[0, 0])
    product = g[2, 3] + s * (g[2, 2] + g[1, 3] + s * g[1, 2] + t * g[1, 1])
    product = product + t * (g[1, 2] + g[0, 3] + s * g[0, 2] + t * g[0, 1])
    b2 = 1.0 - product / squares
    for k, b in enumerate((b0, b1, b2)):
        en_ref[0:1, k:k + 1] = SHIFT + b * (1.0 / RATE)
    one, two, three = s + b2, t + s * b2, t * b2
    for q in range(NCH):
        known = one * ys[2][:, columns(q)] + two * ys[1][:, columns(q)] + three * ys[0][:, columns(q)]
        out_ref[0, :, columns(q)] = ys[3][:, columns(q)] + known
    pltpu.make_async_copy(every, every, sum_sems.at[0]).wait()


def shards(wave, diagonal, left_env, right_env, pair_hop, segs, nblk):
    zg = nblk // XG
    dma = pltpu.SemaphoreType.DMA
    square = pltpu.VMEM((BS, BS), F32)
    vmem = pl.BlockSpec(memory_space=pltpu.VMEM)
    given = [pltpu.with_memory_space_constraint(a, pltpu.HBM) for a in (pair_hop, wave, diagonal, left_env, right_env)]
    return pl.pallas_call(
        functools.partial(kernel, segs, nblk),
        out_shape=(
            jax.ShapeDtypeStruct((1, BS, BS), F32),
            jax.ShapeDtypeStruct((1, ITERS), F32),
        ),
        in_specs=[pl.BlockSpec(memory_space=pl.ANY)] * 5,
        out_specs=(vmem, vmem),
        scratch_shapes=[square] * (ITERS + 1) + [pltpu.VMEM((3, BS, CW), BF16)] * (ITERS * NCH) + [
            pltpu.SMEM((2,), jnp.int32),
            pltpu.VMEM((BS, BS), BF16),
            pltpu.VMEM((2, BS, BS), BF16),
            pltpu.VMEM((2, BS, BS), BF16),
            pltpu.VMEM((2, BS, BS), BF16),
            square, square,
            pltpu.VMEM((nblk, 1, CW), F32),
            dma((NCH + 3,)),
            dma((4,)),
            dma((4,)),
            dma((ITERS, NCH, 2)),
            dma((ITERS, NCH, 2)),
            dma((2,)),
            pltpu.SemaphoreType.REGULAR((zg.bit_length() - 1,)),
        ],
        compiler_params=pltpu.CompilerParams(
            collective_id=0, has_side_effects=True, vmem_limit_bytes=48 * 2 ** 20),
        cost_estimate=pl.CostEstimate(flops=ITERS * 8 * BS ** 3, bytes_accessed=9 * 2 ** 19, transcendentals=0),
    )(*given)


def solution(mesh):
    placed = (
        P("chain", "block", None),
        P("chain", "block", None),
        P("chain", "block", None, None),
        P("chain", "block", None, None),
        P("block"),
    )
    return jax.shard_map(
        functools.partial(shards, segs=mesh.shape["chain"], nblk=mesh.shape["block"]),
        mesh=mesh,
        in_specs=placed,
        out_specs=(P("chain", "block", None), P("chain", None)),
        check_vma=False,
    )
```

time: 92.7 us -> 67.7 us (0.73)
  Pallas kernels: 84.9 us -> 65.5 us
  local copies, waits for them, and re-layouts: 6.84 us -> 1.48 us
    pallas_call x1, Pallas kernels: 84.9 us -> 65.5 us  [shards(): pl.pallas_call(functools.partial(kernel, segs, nblk), out_shape=(jax.Shap...]
    unnamed x12 -> x2, local copies, waits for them, and re-layouts: 6.84 us -> 1.48 us
where the time goes in v2:
time: 67.7 us; the launch traced here: 67.6 us
  Pallas kernels  65.5 us (97%)
  local copies, waits for them, and re-layouts  1.48 us (2%)
    pallas_call x1, Pallas kernels, shards(): pl.pallas_call(functools.partial(kernel, segs, nblk), out_shape=(jax.Shap...  65.5 us
    unnamed x2, local copies, waits for them, and re-layouts  1.48 us

profile of v2, /device:TPU:24, one launch (start us, length us, event | category | flops | bytes accessed | tf_op | source)
XLA Modules:
  0.0 67.6 jit_solution(13698657495789067208)
XLA Ops:
  0.6 65.5 %shard_map.68 = (f32[1,512,512]{2,1,0:T(8,128)S(1)}, f32[1,3]{1,0:T(1,128)S(1)}) custom-call(s32[2]{0:T(128)} %refs_0_.1, f32[1,512,512]{2,1,0:T(8,128)} %refs_1_.1, bf16[1,512,512]{2,1,0:T(8,128)(2,1)} %refs_2_.1, bf16[1,2,512,512]{3,2,1,0:T(8,128)(2,1)} %refs_3_.1, bf16[1,2,512,512]{3,2,1,0:T(8,128)(2,1)} %refs_4_.1), custom_call_target="tpu_custom_call" | custom-call | flops 3221225472 | bytes 4718592 | tf_op jit(solution)/shard_map/pallas_call | solution.py:257
  66.1 1.0 %copy.9 = f32[1,512,512]{2,1,0:T(8,128)} copy(f32[1,512,512]{2,1,0:T(8,128)S(1)} %get-tuple-element.4) | data formatting | bytes 2097152
  67.1 0.5 copy.10

commit v3 on v2

--- a/solution.py
+++ b/solution.py
@@ -110,11 +110,19 @@
     pl.semaphore_wait(barrier, len(partners))
     for copy in l_copies:
         copy.start()
+
+    def send_first(chunks):
+        for q in chunks:
+            for copy in moves[0][q]:
+                copy.start()
+
     for q in range(NCH):
         wave_in[q].wait()
         bufs[q][1] = ys[0][:, columns(q)].astype(BF16)
-        for copy in moves[0][q]:
-            copy.start()
+        if q == 0:
+            send_first([q])
+        else:
+            pl.when(jnp.logical_not(even))(functools.partial(send_first, [q]))
     near_start(0)
 
     hop_in.wait()
@@ -127,6 +135,9 @@
         rt_v[p] = rights.T.astype(BF16)
     diag_in.wait()
 
+    l_copies[0].wait_recv()
+    pl.when(even)(functools.partial(send_first, range(1, NCH)))
+
     for q in range(NCH):
         m_v[:, columns(q)] = (1.0 + RATE * SHIFT) - RATE * diag_v[:, columns(q)].astype(F32)
 
@@ -169,7 +180,8 @@
         if k == 0:
             for s in range(NCH - 1):
                 arrived(0, s)
-                l_copies[s].wait_recv()
+                if s > 0:
+                    l_copies[s].wait_recv()
                 near_next(s)
                 for t in range(s + 1):
                     first_terms(t, range(s + 1) if t == s else [s], t == s and s < 2)
@@ -217,7 +229,7 @@
                         last_sums[a] += fold(ys[a][:, columns(q)] * y)
         if k < ITERS - 1:
             for pair in PAIRS:
-                if pair[1] == k + 1 or (k == 0 and pair == (0, 0)):
+                if pair[1] == k + 1 or (k, pair) == (0, (0, 0)):
                     row = row + placed(pair, inner(*pair))
     for r in range(NCH - 1, len(reaches)):
         near_next(r)

time: 67.7 us -> 66 us (0.975)
  Pallas kernels: 65.5 us -> 63.8 us
    pallas_call x1, Pallas kernels: 65.5 us -> 63.8 us  [shards(): pl.pallas_call(functools.partial(kernel, segs, nblk), out_shape=(jax.Shap...]
where the time goes in v3:
time: 66 us; the launch traced here: 65.9 us
  Pallas kernels  63.8 us (97%)
  local copies, waits for them, and re-layouts  1.48 us (2%)
    pallas_call x1, Pallas kernels, shards(): pl.pallas_call(functools.partial(kernel, segs, nblk), out_shape=(jax.Shap...  63.8 us
    unnamed x2, local copies, waits for them, and re-layouts  1.48 us

profile of v3, /device:TPU:24, one launch (start us, length us, event | category | flops | bytes accessed | tf_op | source)
XLA Modules:
  0.0 65.9 jit_solution(239858816099636107)
XLA Ops:
  0.6 63.8 %shard_map.68 = (f32[1,512,512]{2,1,0:T(8,128)S(1)}, f32[1,3]{1,0:T(1,128)S(1)}) custom-call(s32[2]{0:T(128)} %refs_0_.1, f32[1,512,512]{2,1,0:T(8,128)} %refs_1_.1, bf16[1,512,512]{2,1,0:T(8,128)(2,1)} %refs_2_.1, bf16[1,2,512,512]{3,2,1,0:T(8,128)(2,1)} %refs_3_.1, bf16[1,2,512,512]{3,2,1,0:T(8,128)(2,1)} %refs_4_.1), custom_call_target="tpu_custom_call" | custom-call | flops 3221225472 | bytes 4718592 | tf_op jit(solution)/shard_map/pallas_call | solution.py:269
  64.4 1.0 %copy.9 = f32[1,512,512]{2,1,0:T(8,128)} copy(f32[1,512,512]{2,1,0:T(8,128)S(1)} %get-tuple-element.4) | data formatting | bytes 2097152
  65.4 0.5 copy.10

commit v4 on v3

--- a/solution.py
+++ b/solution.py
@@ -48,13 +48,6 @@
     def block_at(dz, dx):
         return {"block": (zi + dz) % zg * XG + (xi + dx) % XG}
 
-    def far(offset):
-        dz, dx = offset
-        return min(dz, zg - dz) + min(dx, XG - dx)
-
-    others = [(dz, dx) for dz in range(zg) for dx in range(XG) if (dz, dx) != (0, 0)]
-    others = sorted(others, key=far, reverse=True)
-
     barrier = pltpu.get_barrier_semaphore()
     partners = [{"block": up}, {"block": down}] + [block_at(0, dx) for dx in range(1, XG)]
     partners += [block_at(1, 0), block_at(zg - 1, 0), {"chain": after}, {"chain": before}]
@@ -86,11 +79,15 @@
     diag_in = load(diag_hbm.at[0], diag_v, NCH + 1)
     hop_in = load(hop_hbm, hop_s, NCH + 2)
 
+    half = BS // 2
+    pieces = [(0, 0, half), (0, half, half), (1, 0, half), (1, half, half - 64), (1, BS - 64, 64)]
+
     def piece(s):
-        return s // 2, pl.ds((s % 2) * (BS // 2), BS // 2)
+        p, start, size = pieces[s]
+        return p, pl.ds(start, size)
 
     l_copies = []
-    for s in range(4):
+    for s in range(len(pieces)):
         p, rows = piece(s)
         l_copies.append(pltpu.make_async_remote_copy(
             src_ref=left_hbm.at[0, p, rows], dst_ref=left_v.at[p, rows],
@@ -157,10 +154,11 @@
 
     def sums_start(row):
         parts[j] = row
-        for dz, dx in others:
+        for t in range(nblk - 1):
+            other = t + (t >= j).astype(jnp.int32)
             pltpu.make_async_remote_copy(
                 src_ref=parts.at[j], dst_ref=parts.at[j], send_sem=sum_sems.at[0], recv_sem=sum_sems.at[1],
-                device_id=block_at(dz, dx), device_id_type=MESH).start()
+                device_id={"block": other}, device_id_type=MESH).start()
 
     def arrived(k, q):
         for copy in moves[k][q]:
@@ -191,15 +189,17 @@
                 arrived(0, NCH - 1)
                 for t in range(NCH - 1):
                     first_terms(t, [NCH - 1])
-                l_copies[NCH - 1].wait_recv()
-                first_terms(NCH - 1, range(NCH))
+                for t in range(NCH - 1, len(pieces)):
+                    l_copies[t].wait_recv()
+                    first_terms(t, range(NCH))
 
             @pl.when(jnp.logical_not(even))
             def _():
-                l_copies[NCH - 1].wait_recv()
-                first_terms(NCH - 1, range(NCH - 1))
+                for t in range(NCH - 1, len(pieces)):
+                    l_copies[t].wait_recv()
+                    first_terms(t, range(NCH - 1))
                 arrived(0, NCH - 1)
-                for t in range(NCH):
+                for t in range(len(pieces)):
                     first_terms(t, [NCH - 1])
 
         else:
@@ -212,21 +212,19 @@
                     break
                 more = dot(first, jnp.concatenate([rt_v[p, columns(q)] for p in range(2)], axis=0))
                 d_v[...] = more if q == 0 else d_v[...] + more
-        for half in range(2):
-            wide = pl.ds(half * 2 * CW, 2 * CW)
+        for q in range(NCH):
+            d = d_v[:, columns(q)]
             if last is not None:
-                rights = jnp.concatenate([rt_v[p, columns(NCH - 1), wide] for p in range(2)], axis=0)
-                d_v[:, wide] = d_v[:, wide] + dot(last, rights)
-            for q in (2 * half, 2 * half + 1):
-                y = m_v[:, columns(q)] * ys[k][:, columns(q)] - RATE * d_v[:, columns(q)]
-                ys[k + 1][:, columns(q)] = y
-                if k < ITERS - 1:
-                    bufs[(k + 1) * NCH + q][1] = y.astype(BF16)
-                    for copy in moves[k + 1][q]:
-                        copy.start()
-                else:
-                    for a in range(ITERS):
-                        last_sums[a] += fold(ys[a][:, columns(q)] * y)
+                d = d + dot(last, jnp.concatenate([rt_v[p, columns(NCH - 1), columns(q)] for p in range(2)], axis=0))
+            y = m_v[:, columns(q)] * ys[k][:, columns(q)] - RATE * d
+            ys[k + 1][:, columns(q)] = y
+            if k < ITERS - 1:
+                bufs[(k + 1) * NCH + q][1] = y.astype(BF16)
+                for copy in moves[k + 1][q]:
+                    copy.start()
+            else:
+                for a in range(ITERS):
+                    last_sums[a] += fold(ys[a][:, columns(q)] * y)
         if k < ITERS - 1:
             for pair in PAIRS:
                 if pair[1] == k + 1 or (k, pair) == (0, (0, 0)):
@@ -283,8 +281,8 @@
             square, square,
             pltpu.VMEM((nblk, 1, CW), F32),
             dma((NCH + 3,)),
-            dma((4,)),
-            dma((4,)),
+            dma((5,)),
+            dma((5,)),
             dma((ITERS, NCH, 2)),
             dma((ITERS, NCH, 2)),
             dma((2,)),

time: 66 us -> 66.1 us (level)
  no operation moved by 1% of the time
where the time goes in v4:
time: 66.1 us; the launch traced here: 66 us
  Pallas kernels  63.9 us (97%)
  local copies, waits for them, and re-layouts  1.48 us (2%)
    pallas_call x1, Pallas kernels, shards(): pl.pallas_call(functools.partial(kernel, segs, nblk), out_shape=(jax.Shap...  63.9 us
    unnamed x2, local copies, waits for them, and re-layouts  1.48 us

profile of v4, /device:TPU:24, one launch (start us, length us, event | category | flops | bytes accessed | tf_op | source)
XLA Modules:
  0.0 66.0 jit_solution(5829679044382169265)
XLA Ops:
  0.6 63.9 %shard_map.68 = (f32[1,512,512]{2,1,0:T(8,128)S(1)}, f32[1,3]{1,0:T(1,128)S(1)}) custom-call(s32[2]{0:T(128)} %refs_0_.1, f32[1,512,512]{2,1,0:T(8,128)} %refs_1_.1, bf16[1,512,512]{2,1,0:T(8,128)(2,1)} %refs_2_.1, bf16[1,2,512,512]{3,2,1,0:T(8,128)(2,1)} %refs_3_.1, bf16[1,2,512,512]{3,2,1,0:T(8,128)(2,1)} %refs_4_.1), custom_call_target="tpu_custom_call" | custom-call | flops 3221225472 | bytes 4718592 | tf_op jit(solution)/shard_map/pallas_call | solution.py:267
  64.5 1.0 %copy.9 = f32[1,512,512]{2,1,0:T(8,128)} copy(f32[1,512,512]{2,1,0:T(8,128)S(1)} %get-tuple-element.4) | data formatting | bytes 2097152
  65.5 0.5 copy.10

commit v5 on v2

--- a/solution.py
+++ b/solution.py
@@ -55,21 +55,37 @@
     others = [(dz, dx) for dz in range(zg) for dx in range(XG) if (dz, dx) != (0, 0)]
     others = sorted(others, key=far, reverse=True)
 
+    has_up, has_down = j < nblk - 1, j > 0
+
+    def one_if(condition):
+        return jnp.where(condition, 1, 0)
+
+    def signal(semaphore, device):
+        pl.semaphore_signal(semaphore, inc=1, device_id=device, device_id_type=MESH)
+
     barrier = pltpu.get_barrier_semaphore()
-    partners = [{"block": up}, {"block": down}] + [block_at(0, dx) for dx in range(1, XG)]
-    partners += [block_at(1, 0), block_at(zg - 1, 0), {"chain": after}, {"chain": before}]
-    for device in partners:
-        pl.semaphore_signal(barrier, inc=1, device_id=device, device_id_type=MESH)
+    fixed = [block_at(0, dx) for dx in range(1, XG)] + [{"chain": after}, {"chain": before}]
+    for device in fixed:
+        signal(barrier, device)
+    ends = [(has_up, {"block": up}), (has_down, {"block": down})]
+    ends += [(zi < zg - 1, block_at(1, 0)), (zi > 0, block_at(zg - 1, 0))]
+    for condition, device in ends:
+        pl.when(condition)(functools.partial(signal, barrier, device))
+    entered = len(fixed) + sum(one_if(condition) for condition, _ in ends)
 
     reaches = [1 << r for r in range(zg.bit_length() - 1)]
 
+    def near_ends(r):
+        reach = reaches[r]
+        return [(zi < zg - reach, block_at(reach, 0)), (zi >= reach, block_at(zg - reach, 0))]
+
     def near_start(r):
-        for dz in {reaches[r], zg - reaches[r]}:
-            pl.semaphore_signal(near_sem.at[r], inc=1, device_id=block_at(dz, 0), device_id_type=MESH)
+        for condition, device in near_ends(r):
+            pl.when(condition)(functools.partial(signal, near_sem.at[r], device))
 
     def near_next(r):
         if r < len(reaches):
-            pl.semaphore_wait(near_sem.at[r], len({reaches[r], zg - reaches[r]}))
+            pl.semaphore_wait(near_sem.at[r], sum(one_if(condition) for condition, _ in near_ends(r)))
         if r + 1 < len(reaches):
             near_start(r + 1)
 
@@ -89,12 +105,14 @@
     def piece(s):
         return s // 2, pl.ds((s % 2) * (BS // 2), BS // 2)
 
-    l_copies = []
-    for s in range(4):
-        p, rows = piece(s)
-        l_copies.append(pltpu.make_async_remote_copy(
+    def left_copy(index, p, rows):
+        return pltpu.make_async_remote_copy(
             src_ref=left_hbm.at[0, p, rows], dst_ref=left_v.at[p, rows],
-            send_sem=l_send.at[s], recv_sem=l_recv.at[s], device_id={"chain": after}, device_id_type=MESH))
+            send_sem=l_send.at[index], recv_sem=l_recv.at[index], device_id={"chain": after}, device_id_type=MESH)
+
+    head = 32
+    l_head = left_copy(4, 0, pl.ds(0, head))
+    l_copies = [left_copy(0, 0, pl.ds(head, BS // 2 - head))] + [left_copy(s, *piece(s)) for s in range(1, 4)]
 
     def exchange(k, q):
         buf = bufs[k * NCH + q]
@@ -107,25 +125,41 @@
 
     moves = [[exchange(k, q) for q in range(NCH)] for k in range(ITERS)]
 
-    pl.semaphore_wait(barrier, len(partners))
-    for copy in l_copies:
+    pl.semaphore_wait(barrier, entered)
+    for copy in [l_head] + l_copies:
         copy.start()
+
+    def send(k, chunks):
+        for way, condition in enumerate((has_up, has_down)):
+            @pl.when(condition)
+            def _():
+                for q in chunks:
+                    moves[k][q][way].start()
+
     for q in range(NCH):
         wave_in[q].wait()
         bufs[q][1] = ys[0][:, columns(q)].astype(BF16)
-        for copy in moves[0][q]:
-            copy.start()
+        if q < 0:
+            send(0, [q])
+    pl.when(jnp.logical_not(even))(functools.partial(send, 0, range(0, NCH)))
     near_start(0)
 
     hop_in.wait()
     hops = [hop_s[p] for p in range(2)]
     right_in.wait()
     for p in range(2):
-        source = j + hops[p] - 1
-        inside = jnp.logical_and(source >= 0, source < nblk)
-        rights = right_v[p].astype(F32) * jnp.where(inside, 1.0, 0.0).astype(F32)
-        rt_v[p] = rights.T.astype(BF16)
+        rt_v[p] = right_v[p].astype(F32).T.astype(BF16)
+
+    def blank(slot):
+        for buf in bufs:
+            buf[slot] = jnp.zeros((BS, CW), BF16)
+
+    pl.when(jnp.logical_not(has_down))(functools.partial(blank, 0))
+    pl.when(jnp.logical_not(has_up))(functools.partial(blank, 2))
     diag_in.wait()
+
+    l_head.wait_recv()
+    pl.when(even)(functools.partial(send, 0, range(0, NCH)))
 
     for q in range(NCH):
         m_v[:, columns(q)] = (1.0 + RATE * SHIFT) - RATE * diag_v[:, columns(q)].astype(F32)
@@ -152,8 +186,8 @@
                 device_id=block_at(dz, dx), device_id_type=MESH).start()
 
     def arrived(k, q):
-        for copy in moves[k][q]:
-            copy.wait_recv()
+        for way, condition in enumerate((has_down, has_up)):
+            pl.when(condition)(moves[k][q][way].wait_recv)
 
     def first_terms(t, chunks, begin=False):
         p, rows = piece(t)
@@ -170,9 +204,10 @@
             for s in range(NCH - 1):
                 arrived(0, s)
                 l_copies[s].wait_recv()
-                near_next(s)
                 for t in range(s + 1):
                     first_terms(t, range(s + 1) if t == s else [s], t == s and s < 2)
+
+            near_next(0)
 
             @pl.when(even)
             def _():
@@ -192,6 +227,8 @@
 
         else:
             for q in range(NCH):
+                if (k, q) in ((1, 0), (1, NCH - 1)):
+                    near_next(1 if q == 0 else 2)
                 arrived(k, q)
                 first = [dot(left_v[p], bufs[k * NCH + q][hops[p]]).astype(BF16) for p in range(2)]
                 first = jnp.concatenate(first, axis=1)
@@ -210,22 +247,28 @@
                 ys[k + 1][:, columns(q)] = y
                 if k < ITERS - 1:
                     bufs[(k + 1) * NCH + q][1] = y.astype(BF16)
-                    for copy in moves[k + 1][q]:
-                        copy.start()
                 else:
                     for a in range(ITERS):
                         last_sums[a] += fold(ys[a][:, columns(q)] * y)
+            if k < ITERS - 1:
+                send(k + 1, (2 * half, 2 * half + 1))
         if k < ITERS - 1:
             for pair in PAIRS:
                 if pair[1] == k + 1 or (k == 0 and pair == (0, 0)):
                     row = row + placed(pair, inner(*pair))
-    for r in range(NCH - 1, len(reaches)):
+    for r in range(3, len(reaches)):
         near_next(r)
     for a in range(ITERS):
         row = row + placed((a, ITERS), last_sums[a])
     sums_start(row)
-    for copy in l_copies + [m for step in moves for pair in step for m in pair]:
+    for copy in [l_head] + l_copies:
         copy.wait_send()
+    for way, condition in enumerate((has_up, has_down)):
+        @pl.when(condition)
+        def _():
+            for step in moves:
+                for pair in step:
+                    pair[way].wait_send()
     pltpu.make_async_copy(every, every, sum_sems.at[1]).wait()
     total = jnp.sum(parts[...], axis=0)
     g = {}
@@ -271,8 +314,8 @@
             square, square,
             pltpu.VMEM((nblk, 1, CW), F32),
             dma((NCH + 3,)),
-            dma((4,)),
-            dma((4,)),
+            dma((5,)),
+            dma((5,)),
             dma((ITERS, NCH, 2)),
             dma((ITERS, NCH, 2)),
             dma((2,)),

time: 67.7 us -> 66 us (0.975)
  Pallas kernels: 65.5 us -> 63.2 us
    pallas_call x1, Pallas kernels: 65.5 us -> 63.2 us  [shards(): pl.pallas_call(functools.partial(kernel, segs, nblk), out_shape=(jax.Shap...]
where the time goes in v5:
time: 66 us; the launch traced here: 65.4 us
  Pallas kernels  63.2 us (96%)
  local copies, waits for them, and re-layouts  1.48 us (2%)
    pallas_call x1, Pallas kernels, shards(): pl.pallas_call(functools.partial(kernel, segs, nblk), out_shape=(jax.Shap...  63.2 us
    unnamed x2, local copies, waits for them, and re-layouts  1.48 us

profile of v5, /device:TPU:24, one launch (start us, length us, event | category | flops | bytes accessed | tf_op | source)
XLA Modules:
  0.0 65.4 jit_solution(13409644889078428937)
XLA Ops:
  0.6 63.2 %shard_map.68 = (f32[1,512,512]{2,1,0:T(8,128)S(1)}, f32[1,3]{1,0:T(1,128)S(1)}) custom-call(s32[2]{0:T(128)} %refs_0_.1, f32[1,512,512]{2,1,0:T(8,128)} %refs_1_.1, bf16[1,512,512]{2,1,0:T(8,128)(2,1)} %refs_2_.1, bf16[1,2,512,512]{3,2,1,0:T(8,128)(2,1)} %refs_3_.1, bf16[1,2,512,512]{3,2,1,0:T(8,128)(2,1)} %refs_4_.1), custom_call_target="tpu_custom_call" | custom-call | flops 3221225472 | bytes 4718592 | tf_op jit(solution)/shard_map/pallas_call | solution.py:300
  63.9 1.0 %copy.9 = f32[1,512,512]{2,1,0:T(8,128)} copy(f32[1,512,512]{2,1,0:T(8,128)S(1)} %get-tuple-element.4) | data formatting | bytes 2097152
  64.8 0.5 copy.10
